TPU v7x, 32 devices: a whole 2x2x4 slice. The times are simulated.
32 devices in a mesh: row: 4 (over y, core), col: 8 (over z, x).
Axes of the slice: x: 2, y: 2, z: 4, core: 2. Of those that a mesh axis runs over, the one named last changes fastest.
Arguments:
- latent: bfloat16 [4, 16, 32, 320], P(None, 'row', 'col'), may hold values from -6 to 6
- conv_weight: bfloat16 [2, 3, 3, 320, 320], replicated, may hold values from -0.109375 to 0.109375
- conv_gain: float32 [2, 320], replicated, may hold values from 0.25 to 1.75
- qkv_weight: bfloat16 [3, 512, 320], P(None, 'col'), may hold values from -0.3125 to 0.3125
- qk_gain: bfloat16 [2, 512], P(None, 'col'), may hold values from 0.6 to 9, as said below
- out_weight: bfloat16 [512, 320], P('col'), may hold values from -0.5 to 0.5
Outputs:
- features: bfloat16 [4, 16, 32, 320], P(None, 'row', 'col')
- mixed: bfloat16 [4, 8, 16, 320], P('row', None, 'col')
Inputs may be any that keep to these rules, and one draw needn't show every extreme that they name: `qk_gain`: positive gains.
All inputs are finite; a program needn't handle non-finite values.
Results may differ from a plain program's by a relative error of at most 0.035.
Values may be sent and summed in bfloat16 or wider, within the bound.
A program may use at most 64 MiB of HBM per device.

v0:
```python
import math

import jax
import jax.numpy as jnp
from jax import lax
from jax.sharding import PartitionSpec as P


def with_halo(array, sides, width):
    for axis, dim in sides:
        size, length = (lax.axis_size(axis), array.shape[dim])
        up = [(i, (i + 1) % size) for i in range(size)]
        down = [(j, i) for i, j in up]
        last = lax.slice_in_dim(array, length - width, length, axis=dim)
        leading = lax.slice_in_dim(array, 0, width, axis=dim)
        before = lax.ppermute(last, axis, up)
        after = lax.ppermute(leading, axis, down)
        array = jnp.concatenate([before, array, after], axis=dim)
    return array


def from_partner(array, axis, bit):
    return lax.ppermute(array, axis, [(i, i ^ 1 << bit) for i in range(lax.axis_size(axis))])


def rms_silu(hidden, gain_row):
    factor = lax.rsqrt(jnp.mean(hidden * hidden, axis=-1, keepdims=True) + 1e-06)
    return jax.nn.silu(hidden * factor * gain_row).astype(jnp.bfloat16)


def conv_taps(padded, kernels, out_rows, out_cols):
    image_count = padded.shape[0]
    channels = padded.shape[-1]
    total = jnp.zeros((image_count * out_rows * out_cols, kernels.shape[-1]), jnp.float32)
    for row_tap in range(3):
        for col_tap in range(3):
            window = padded[:, row_tap : row_tap + out_rows, col_tap : col_tap + out_cols]
            total = total + jnp.dot(
                window.reshape(image_count * out_rows * out_cols, channels),
                kernels[row_tap, col_tap],
                preferred_element_type=jnp.float32,
            )
    return total.reshape(image_count, out_rows, out_cols, kernels.shape[-1])


def head_norm(projected, gain_row):
    factor = lax.rsqrt(jnp.mean(projected * projected, axis=-1, keepdims=True) + 1e-06)
    return (projected * factor * gain_row.astype(jnp.float32)).astype(jnp.bfloat16)


def project(source, matrix):
    return lax.dot_general(
        source, matrix, (((1,), (1,)), ((), ())), preferred_element_type=jnp.float32
    )


def shards(latent, conv_weight, conv_gain, qkv_weight, qk_gain, out_weight):
    image_count, rows_tile, cols_tile, channels = latent.shape
    layer_count = conv_weight.shape[0]
    col_count = lax.axis_size("col")
    half_bit = lax.axis_index("col") % 2
    hidden = with_halo(latent, (("row", 1), ("col", 2)), layer_count)
    for layer_index in range(layer_count):
        activation = rms_silu(hidden.astype(jnp.float32), conv_gain[layer_index])
        inner_rows = hidden.shape[1] - 2
        inner_cols = hidden.shape[2] - 2
        conv_sum = conv_taps(activation, conv_weight[layer_index], inner_rows, inner_cols)
        hidden = (hidden[:, 1:-1, 1:-1].astype(jnp.float32) + conv_sum).astype(jnp.bfloat16)
    tok_rows = rows_tile // 2
    tok_cols = cols_tile // 2
    pooled = (
        hidden.astype(jnp.float32)
        .reshape(image_count, tok_rows, 2, tok_cols, 2, channels)
        .mean(axis=(2, 4))
        .astype(jnp.bfloat16)
    )
    own_strip = lax.all_to_all(pooled, "row", split_axis=0, concat_axis=1, tiled=True)[0]
    image_tok = lax.all_gather(own_strip, "col", axis=1, tiled=True)
    partner_parts = from_partner((qkv_weight, qk_gain, out_weight), "col", 0)

    def join_halves(own_part, far_part, dim):
        lower_part = jnp.where(half_bit == 0, own_part, far_part)
        upper_part = jnp.where(half_bit == 0, far_part, own_part)
        return jnp.concatenate((lower_part, upper_part), dim)

    head_weight = join_halves(qkv_weight, partner_parts[0], 1)
    head_gain = join_halves(qk_gain, partner_parts[1], 1)
    head_out = join_halves(out_weight, partner_parts[2], 0)
    head_dim = head_weight.shape[1]
    scale = head_dim ** (-0.5)
    all_rows = image_tok.shape[0]
    all_tokens = image_tok.reshape(-1, channels)
    split_view = image_tok.reshape(all_rows, col_count, 2, tok_cols // 2, channels)
    own_tokens = lax.dynamic_index_in_dim(split_view, half_bit, 2, keepdims=False).reshape(
        -1, channels
    )
    own_count = own_tokens.shape[0]
    query_norm = head_norm(project(own_tokens, head_weight[0]), head_gain[0])
    key_norm = head_norm(project(all_tokens, head_weight[1]), head_gain[1])
    value_rows = project(all_tokens, head_weight[2]).astype(jnp.bfloat16)
    block_rows = math.gcd(own_count, 512)

    def one_block(query_block):
        scores = project(query_block, key_norm) * scale
        shifted = jnp.exp(scores - jnp.max(scores, axis=1, keepdims=True))
        return jnp.dot(
            shifted.astype(jnp.bfloat16), value_rows, preferred_element_type=jnp.float32
        ) / jnp.sum(shifted, axis=1, keepdims=True)

    attended = lax.map(one_block, query_norm.reshape(own_count // block_rows, block_rows, head_dim))
    attended = attended.reshape(own_count, head_dim).astype(jnp.bfloat16)
    head_terms = jnp.dot(attended, head_out, preferred_element_type=jnp.float32)
    head_terms = head_terms.reshape(all_rows, col_count, tok_cols // 2, channels)
    returned = lax.all_to_all(
        head_terms.astype(jnp.bfloat16), "col", split_axis=1, concat_axis=1, tiled=True
    ).astype(head_terms.dtype)
    summed = returned.reshape(all_rows, col_count // 2, 2, tok_cols // 2, channels).sum(axis=1)
    summed = summed.reshape(all_rows, tok_cols, channels)
    mixed = (own_strip.astype(jnp.float32) + summed).astype(jnp.bfloat16)
    return (hidden, mixed[None])


def solution(mesh):
    placed = (
        P(None, "row", "col", None),
        P(),
        P(),
        P(None, "col", None),
        P(None, "col"),
        P("col", None),
    )
    return jax.shard_map(
        shards,
        mesh=mesh,
        in_specs=placed,
        out_specs=(P(None, "row", "col", None), P("row", None, "col", None)),
        check_vma=False,
    )
```

profile of v0, /device:TPU:0, one launch (start us, length us, event | category | flops | bytes accessed | tf_op | source)
XLA Modules:
  0.0 90.6 jit_solution(15382116381084642659)
XLA Ops:
  0.6 0.8 fusion.58
  1.4 0.5 collective-permute-start
  1.9 2.0 %collective-permute-start.1 = (bf16[4,2,4,320]{3,2,1,0:T(4,128)(2,1)S(1)}, bf16[4,2,4,320]{3,2,1,0:T(4,128)(2,1)S(1)}, u32[]{:S(2)}, u32[]{:S(2)}) collective-permute-start(bf16[4,2,4,320]{3,2,1,0:T(4,128)(2,1)S(1)} %get-tuple-element.53), channel_id=1, source_target_pairs={{8,0},{16,8},{24,16},{0,24},{9,1},{17,9},{25,17},{1,25},{10,2},{18... | collective-permute-start | bytes 61448 | tf_op jit(solution)/shard_map/ppermute | solution.py:17
  3.9 2.2 %collective-permute-start.4 = (bf16[3,64,320]{2,1,0:T(8,128)(2,1)}, bf16[3,64,320]{2,1,0:T(8,128)(2,1)}, u32[]{:S(2)}, u32[]{:S(2)}) collective-permute-start(bf16[3,64,320]{2,1,0:T(8,128)(2,1)} %param.9), channel_id=1, source_target_pairs={{0,1},{1,0},{2,3},{3,2},{4,5},{5,4},{6,7},{7,6},{8,9},{9,8},{10,11... | collective-permute-start | bytes 368648 | tf_op jit(solution)/shard_map/ppermute | solution.py:23
  6.2 1.5 %copy.63 = bf16[64,320]{0,1:T(8,128)(2,1)} copy(bf16[64,320]{1,0:T(8,128)(2,1)} %param.11) | data formatting | bytes 81920 | tf_op args[5]
  7.7 2.0 %collective-permute-start.6 = (bf16[64,320]{0,1:T(8,128)(2,1)}, bf16[64,320]{0,1:T(8,128)(2,1)}, u32[]{:S(2)}, u32[]{:S(2)}) collective-permute-start(bf16[64,320]{0,1:T(8,128)(2,1)} %copy.63), channel_id=1, source_target_pairs={{0,1},{1,0},{2,3},{3,2},{4,5},{5,4},{6,7},{7,6},{8,9},{9,8},{10,11... | collective-permute-start | bytes 122888 | tf_op jit(solution)/shard_map/ppermute | solution.py:23
  9.7 0.8 slice_reduce_fusion
  10.5 4.1 %slice_bitcast_fusion = (bf16[3,3,320,320]{3,2,1,0:T(8,128)(2,1)S(1)}, bf16[3,3,320,320]{3,2,1,0:T(8,128)(2,1)}) fusion(bf16[2,3,3,320,320]{4,3,2,1,0:T(8,128)(2,1)} %param.7), kind=kLoop, calls=%fused_computation | loop fusion | bytes 7372800 | tf_op jit(solution)/shard_map/squeeze | solution.py:67
  14.7 0.1 pad_maximum_fusion.2
  14.8 0.1 fusion.57
  14.9 0.1 collective-permute-start.2
  15.0 4.7 %collective-permute-start.3 = (bf16[4,8,2,320]{3,2,1,0:T(2,128)(2,1)S(1)}, bf16[4,8,2,320]{3,2,1,0:T(2,128)(2,1)S(1)}, u32[]{:S(2)}, u32[]{:S(2)}) collective-permute-start(bf16[4,8,2,320]{3,2,1,0:T(2,128)(2,1)S(1)} %get-tuple-element.52), channel_id=1, source_target_pairs={{1,0},{2,1},{3,2},{4,3},{5,4},{6,5},{7,6},{0,7},{9,8},{10,9},{11,1... | collective-permute-start | bytes 122888 | tf_op jit(solution)/shard_map/ppermute | solution.py:17
  19.7 0.6 bitcast_convert_fusion.1
  20.3 1.5 %collective-permute-done.2 = bf16[4,8,2,320]{3,2,1,0:T(2,128)(2,1)S(1)} collective-permute-done((bf16[4,8,2,320]{3,2,1,0:T(2,128)(2,1)S(1)}, bf16[4,8,2,320]{3,2,1,0:T(2,128)(2,1)S(1)}, u32[]{:S(2)}, u32[]{:S(2)}) %collective-permute-start.2) | collective-permute-done | bytes 40992 | tf_op jit(solution)/shard_map/ppermute | solution.py:16
  21.7 0.3 fusion.5
  22.0 0.2 fusion.12
  22.2 0.8 fusion.55
  23.1 1.6 %reshape.162 = bf16[144,320]{1,0:T(8,128)(2,1)} reshape(bf16[4,6,6,320]{3,2,1,0:T(8,128)(2,1)} %get-tuple-element.39) | data formatting | bytes 184320 | tf_op jit(solution)/shard_map/reshape | solution.py:39
  24.7 1.6 %reshape.163 = bf16[144,320]{1,0:T(8,128)(2,1)} reshape(bf16[4,6,6,320]{3,2,1,0:T(8,128)(2,1)} %get-tuple-element.38) | data formatting | bytes 184320 | tf_op jit(solution)/shard_map/reshape | solution.py:39
  26.3 0.1 reshape.164
  26.4 0.1 reshape.165
  26.5 0.1 reshape.166
  26.5 0.1 reshape.167
  26.6 0.1 reshape.168
  26.7 0.1 reshape.169
  26.8 0.1 reshape.170
  26.9 1.4 %fusion.22 = f32[144,320]{1,0:T(8,128)S(1)} fusion(bf16[144,320]{1,0:T(8,128)(2,1)} %reshape.162, bf16[3,3,320,320]{3,2,1,0:T(8,128)(2,1)} %get-tuple-element.28), kind=kOutput, calls=%fused_computation.70 | convolution fusion | flops 29491200 | bytes 540672 | tf_op jit(solution)/shard_map/dot_general | solution.py:38
  28.2 1.2 %convolution_add_fusion.7 = f32[144,320]{1,0:T(8,128)S(1)} fusion(f32[144,320]{1,0:T(8,128)S(1)} %fusion.22, bf16[144,320]{1,0:T(8,128)(2,1)} %reshape.163, bf16[3,3,320,320]{3,2,1,0:T(8,128)(2,1)} %get-tuple-element.28), kind=kOutput, calls=%fused_computation.9 | convolution fusion | flops 29537280 | bytes 724992 | tf_op jit(solution)/shard_map/dot_general | solution.py:38
  29.5 1.2 %convolution_add_fusion.6 = f32[144,320]{1,0:T(8,128)S(1)} fusion(f32[144,320]{1,0:T(8,128)S(1)} %convolution_add_fusion.7, bf16[144,320]{1,0:T(8,128)(2,1)S(1)} %reshape.164, bf16[3,3,320,320]{3,2,1,0:T(8,128)(2,1)} %get-tuple-element.28), kind=kOutput, calls=%fused_computation.8 | convolution fusion | flops 29537280 | bytes 706560 | tf_op jit(solution)/shard_map/dot_general | solution.py:38
  30.6 1.2 %convolution_add_fusion.5 = f32[144,320]{1,0:T(8,128)S(1)} fusion(f32[144,320]{1,0:T(8,128)S(1)} %convolution_add_fusion.6, bf16[144,320]{1,0:T(8,128)(2,1)S(1)} %reshape.165, bf16[3,3,320,320]{3,2,1,0:T(8,128)(2,1)} %get-tuple-element.28), kind=kOutput, calls=%fused_computation.7 | convolution fusion | flops 29537280 | bytes 706560 | tf_op jit(solution)/shard_map/dot_general | solution.py:38
  31.8 0.2 convolution_add_fusion.4
  32.1 0.2 convolution_add_fusion.3
  32.3 0.2 convolution_add_fusion.2
  32.6 0.2 convolution_add_fusion.1
  32.8 0.2 convolution_add_fusion
  33.1 0.2 fusion.13
  33.3 0.2 fusion.20
  33.4 0.1 fusion.56
  33.8 0.2 fusion.21
  34.0 0.2 convolution_add_fusion.15
  34.2 0.2 convolution_add_fusion.14
  34.4 0.2 convolution_add_fusion.13
  34.6 0.2 convolution_add_fusion.12
  34.7 0.2 convolution_add_fusion.11
  34.9 0.2 convolution_add_fusion.10
  35.1 0.2 convolution_add_fusion.9
  35.3 0.2 convolution_add_fusion.8
  35.6 0.1 reduce_sum.68
  35.7 0.6 copy.55
  36.3 3.3 %all-to-all-start = ((bf16[4,2,2,320]{3,1,2,0:T(2,128)(2,1)}), bf16[4,2,2,320]{3,1,2,0:T(2,128)(2,1)S(1)}, u32[]{:S(2)}, u32[]{:S(2)}) async-start(bf16[4,2,2,320]{3,1,2,0:T(2,128)(2,1)} %copy.55), calls=%async_computation | async-start | bytes 24576 | tf_op jit(solution)/shard_map/all_to_all | solution.py:77
  39.6 0.9 %broadcast_select_fusion.3 = (bf16[64,320]{0,1:T(8,128)(2,1)S(1)}, bf16[64,320]{0,1:T(8,128)(2,1)S(1)}) fusion(bf16[64,320]{0,1:T(8,128)(2,1)} %copy.63, bf16[64,320]{0,1:T(8,128)(2,1)} %collective-permute-done.6, pred[]{:T(512)S(6)} %eq.4), kind=kLoop, calls=%fused_computation.89 | loop fusion | flops 40960 | bytes 163841 | tf_op jit(solution)/shard_map/jit(_where)/select_n | solution.py:82
  40.5 2.8 %all-to-all-done = bf16[4,2,2,320]{3,1,2,0:T(2,128)(2,1)S(1)} async-done(((bf16[4,2,2,320]{3,1,2,0:T(2,128)(2,1)}), bf16[4,2,2,320]{3,1,2,0:T(2,128)(2,1)S(1)}, u32[]{:S(2)}, u32[]{:S(2)}) %all-to-all-start) | async-done | bytes 10272 | tf_op jit(solution)/shard_map/all_to_all | solution.py:77
  43.4 30.6 %all_gather.3 = bf16[8,16,320]{2,0,1:T(8,128)(2,1)S(1)} all-gather(bf16[8,2,320]{2,0,1:T(8,128)(2,1)S(1)} %copy.59), channel_id=1, replica_groups=mesh['row'=4,'col'=8] {'col'}, dimensions={1}, use_global_device_ids=true | all-gather | bytes 92160 | tf_op jit(solution)/shard_map/all_gather | solution.py:78
  74.0 0.9 %broadcast_select_fusion.1 = (bf16[3,64,320]{2,1,0:T(8,128)(2,1)S(1)}, bf16[3,64,320]{2,1,0:T(8,128)(2,1)S(1)}) fusion(bf16[3,64,320]{2,1,0:T(8,128)(2,1)S(1)} %copy-done.3, bf16[3,64,320]{2,1,0:T(8,128)(2,1)} %collective-permute-done.4, pred[]{:T(512)S(6)} %eq.4), kind=kLoop, calls=%fused_computation.73 | loop fusion | flops 122880 | bytes 491521 | tf_op jit(solution)/shard_map/jit(_where)/select_n | solution.py:82
  75.0 0.3 multiply_reduce_fusion.1
  75.2 0.2 multiply_reduce_fusion
  75.5 0.3 fusion.59
  75.8 0.2 fusion.42
  76.0 0.3 fusion.4
  76.3 0.2 fusion
  76.6 0.6 copy.65
  77.2 6.0 %all-to-all-start.1 = ((bf16[8,8,1,320]{3,0,2,1:T(8,128)(2,1)}), bf16[8,8,1,320]{3,0,2,1:T(8,128)(2,1)S(1)}, u32[]{:S(2)}, u32[]{:S(2)}) async-start(bf16[8,8,1,320]{3,0,2,1:T(8,128)(2,1)} %copy.65), calls=%async_computation.1 | async-start | bytes 98304 | tf_op jit(solution)/shard_map/all_to_all | solution.py:114
  83.2 6.8 %all-to-all-done.1 = bf16[8,8,1,320]{3,0,2,1:T(8,128)(2,1)S(1)} async-done(((bf16[8,8,1,320]{3,0,2,1:T(8,128)(2,1)}), bf16[8,8,1,320]{3,0,2,1:T(8,128)(2,1)S(1)}, u32[]{:S(2)}, u32[]{:S(2)}) %all-to-all-start.1) | async-done | bytes 40992 | tf_op jit(solution)/shard_map/all_to_all | solution.py:114
  90.0 0.6 copy.67
  (51 shorter events, 0.7 us)
Async XLA Ops:
  1.4 13.3 %collective-permute-start = (bf16[4,2,4,320]{3,2,1,0:T(4,128)(2,1)S(1)}, bf16[4,2,4,320]{3,2,1,0:T(4,128)(2,1)S(1)}, u32[]{:S(2)}, u32[]{:S(2)}) collective-permute-start(bf16[4,2,4,320]{3,2,1,0:T(4,128)(2,1)S(1)} %get-tuple-element.54), channel_id=1, source_target_pairs={{0,8},{8,16},{16,24},{24,0},{1,9},{9,17},{17,25},{25,1},{2,10},{10... | collective-permute-start | bytes 61448 | tf_op jit(solution)/shard_map/ppermute | solution.py:16
  1.9 12.9 %collective-permute-start.1 = (bf16[4,2,4,320]{3,2,1,0:T(4,128)(2,1)S(1)}, bf16[4,2,4,320]{3,2,1,0:T(4,128)(2,1)S(1)}, u32[]{:S(2)}, u32[]{:S(2)}) collective-permute-start(bf16[4,2,4,320]{3,2,1,0:T(4,128)(2,1)S(1)} %get-tuple-element.53), channel_id=1, source_target_pairs={{8,0},{16,8},{24,16},{0,24},{9,1},{17,9},{25,17},{1,25},{10,2},{18... | collective-permute-start | bytes 61448 | tf_op jit(solution)/shard_map/ppermute | solution.py:17
  3.9 70.1 %collective-permute-start.4 = (bf16[3,64,320]{2,1,0:T(8,128)(2,1)}, bf16[3,64,320]{2,1,0:T(8,128)(2,1)}, u32[]{:S(2)}, u32[]{:S(2)}) collective-permute-start(bf16[3,64,320]{2,1,0:T(8,128)(2,1)} %param.9), channel_id=1, source_target_pairs={{0,1},{1,0},{2,3},{3,2},{4,5},{5,4},{6,7},{7,6},{8,9},{9,8},{10,11... | collective-permute-start | bytes 368648 | tf_op jit(solution)/shard_map/ppermute | solution.py:23
  6.2 8.5 %collective-permute-start.5 = (bf16[2,64]{1,0:T(2,128)(2,1)}, bf16[2,64]{1,0:T(2,128)(2,1)S(1)}, u32[]{:S(2)}, u32[]{:S(2)}) collective-permute-start(bf16[2,64]{1,0:T(2,128)(2,1)} %param.10), channel_id=1, source_target_pairs={{0,1},{1,0},{2,3},{3,2},{4,5},{5,4},{6,7},{7,6},{8,9},{9,8},{10,11... | collective-permute-start | bytes 776 | tf_op jit(solution)/shard_map/ppermute | solution.py:23
  7.7 31.9 %collective-permute-start.6 = (bf16[64,320]{0,1:T(8,128)(2,1)}, bf16[64,320]{0,1:T(8,128)(2,1)}, u32[]{:S(2)}, u32[]{:S(2)}) collective-permute-start(bf16[64,320]{0,1:T(8,128)(2,1)} %copy.63), channel_id=1, source_target_pairs={{0,1},{1,0},{2,3},{3,2},{4,5},{5,4},{6,7},{7,6},{8,9},{9,8},{10,11... | collective-permute-start | bytes 122888 | tf_op jit(solution)/shard_map/ppermute | solution.py:23
  10.5 4.1 %copy-start.6 = (bf16[2,64]{1,0:T(2,128)(2,1)S(1)}, bf16[2,64]{1,0:T(2,128)(2,1)}, u32[]{:S(2)}) copy-start(bf16[2,64]{1,0:T(2,128)(2,1)} %param.10) | copy-start | bytes 772
  10.5 4.2 %copy-start.1 = (bf16[4,4,4,320]{3,2,1,0:T(4,128)(2,1)S(1)}, bf16[4,4,4,320]{3,2,1,0:T(4,128)(2,1)}, u32[]{:S(2)}) copy-start(bf16[4,4,4,320]{3,2,1,0:T(4,128)(2,1)} %param.6) | copy-start | bytes 122884
  14.9 6.8 %collective-permute-start.2 = (bf16[4,8,2,320]{3,2,1,0:T(2,128)(2,1)S(1)}, bf16[4,8,2,320]{3,2,1,0:T(2,128)(2,1)S(1)}, u32[]{:S(2)}, u32[]{:S(2)}) collective-permute-start(bf16[4,8,2,320]{3,2,1,0:T(2,128)(2,1)S(1)} %get-tuple-element.51), channel_id=1, source_target_pairs={{0,1},{1,2},{2,3},{3,4},{4,5},{5,6},{6,7},{7,0},{8,9},{9,10},{10,1... | collective-permute-start | bytes 122888 | tf_op jit(solution)/shard_map/ppermute | solution.py:16
  15.0 6.8 %collective-permute-start.3 = (bf16[4,8,2,320]{3,2,1,0:T(2,128)(2,1)S(1)}, bf16[4,8,2,320]{3,2,1,0:T(2,128)(2,1)S(1)}, u32[]{:S(2)}, u32[]{:S(2)}) collective-permute-start(bf16[4,8,2,320]{3,2,1,0:T(2,128)(2,1)S(1)} %get-tuple-element.52), channel_id=1, source_target_pairs={{1,0},{2,1},{3,2},{4,3},{5,4},{6,5},{7,6},{0,7},{9,8},{10,9},{11,1... | collective-permute-start | bytes 122888 | tf_op jit(solution)/shard_map/ppermute | solution.py:17
  26.8 5.0 %copy-start = (bf16[3,3,320,320]{3,2,1,0:T(8,128)(2,1)S(1)}, bf16[3,3,320,320]{3,2,1,0:T(8,128)(2,1)}, u32[]{:S(2)}) copy-start(bf16[3,3,320,320]{3,2,1,0:T(8,128)(2,1)} %get-tuple-element.28) | copy-start | bytes 5529604
  34.4 39.7 %copy-start.3 = (bf16[3,64,320]{2,1,0:T(8,128)(2,1)S(1)}, bf16[3,64,320]{2,1,0:T(8,128)(2,1)}, u32[]{:S(2)}) copy-start(bf16[3,64,320]{2,1,0:T(8,128)(2,1)} %param.9) | copy-start | bytes 368644
  34.9 40.6 %copy-start.4 = (f32[128]{0:T(128)S(1)}, f32[128]{0:T(128)}, u32[]{:S(2)}) copy-start(f32[128]{0:T(128)} %get-tuple-element.57) | copy-start | bytes 1540
  34.9 40.6 %copy-start.5 = (f32[128]{0:T(128)S(1)}, f32[128]{0:T(128)}, u32[]{:S(2)}) copy-start(f32[128]{0:T(128)} %get-tuple-element.58) | copy-start | bytes 1540
  35.5 55.1 %copy-start.2 = (bf16[4,4,4,320]{3,2,1,0:T(4,128)(2,1)}, bf16[4,4,4,320]{3,2,1,0:T(4,128)(2,1)S(1)}, u32[]{:S(2)}) copy-start(bf16[4,4,4,320]{3,2,1,0:T(4,128)(2,1)S(1)} %add_convert_fusion.1) | copy-start | bytes 122884
  36.3 7.1 %all-to-all-start = ((bf16[4,2,2,320]{3,1,2,0:T(2,128)(2,1)}), bf16[4,2,2,320]{3,1,2,0:T(2,128)(2,1)S(1)}, u32[]{:S(2)}, u32[]{:S(2)}) async-start(bf16[4,2,2,320]{3,1,2,0:T(2,128)(2,1)} %copy.55), calls=%async_computation | async-start | bytes 24576 | tf_op jit(solution)/shard_map/all_to_all | solution.py:77
  77.2 12.8 %all-to-all-start.1 = ((bf16[8,8,1,320]{3,0,2,1:T(8,128)(2,1)}), bf16[8,8,1,320]{3,0,2,1:T(8,128)(2,1)S(1)}, u32[]{:S(2)}, u32[]{:S(2)}) async-start(bf16[8,8,1,320]{3,0,2,1:T(8,128)(2,1)} %copy.65), calls=%async_computation.1 | async-start | bytes 98304 | tf_op jit(solution)/shard_map/all_to_all | solution.py:114
where the time goes:
time: 91.2 us; the launch traced here: 90.6 us
  blocking collectives  30.6 us (34%)
  starting transfers between devices  20.8 us (23%)
  local copies, waits for them, and re-layouts  14.4 us (16%)
  waiting for transfers between devices  11.1 us (12%)
  matrix products  8.97 us (10%)
  other arithmetic  3.73 us (4%)
  between operations  1.1 us (1%)
    all_gather x1, blocking collectives, shards(): image_tok = lax.all_gather(own_strip, 'col', axis=1, tiled=True)  30.6 us
    dot_general x18, matrix products, conv_taps(): jnp.dot(window.reshape(image_count * out_rows * out_cols, channels), kern...  7.63 us
    all_to_all x1, waiting for transfers between devices, shards(): lax.all_to_all(head_terms.astype(jnp.bfloat16), 'col', split_axis=1, conc...  6.76 us
    ppermute x2, starting transfers between devices, with_halo(): after = lax.ppermute(leading, axis, down)  6.71 us
    all_to_all x1, starting transfers between devices, shards(): lax.all_to_all(head_terms.astype(jnp.bfloat16), 'col', split_axis=1, conc...  5.99 us
    ppermute x3, starting transfers between devices, from_partner(): lax.ppermute(array, axis, [(i, i ^ 1 << bit) for i in range(lax.axis_size...  4.24 us
    squeeze x1, local copies, waits for them, and re-layouts, shards(): conv_weight[layer_index]  4.12 us
    reshape x18, local copies, waits for them, and re-layouts, conv_taps(): window.reshape(image_count * out_rows * out_cols, channels)  4.04 us
  transfers between devices with their start and end apart: 9, of which 3 were waited for; matrix products, arithmetic and copies ran while one was open for 25% of the time, Pallas kernels for 0%

commit v1 on v0

v1 whole, which is shorter than its diff:
```python
import functools

import jax
import jax.numpy as jnp
import numpy as np
from jax import lax
from jax.experimental import pallas as pl
from jax.experimental.pallas import tpu as pltpu
from jax.sharding import PartitionSpec as P

MESH = pl.DeviceIdType.MESH
SIDES = [(0, 1), (0, -1), (1, 0), (-1, 0), (1, 1), (1, -1), (-1, 1), (-1, -1)]


def edge_source(step, tile, width):
    return {-1: range(width), 1: range(tile - width, tile), 0: range(tile)}[step]


def edge_target(step, tile, width):
    return {
        -1: range(width + tile, tile + 2 * width),
        1: range(width),
        0: range(width, width + tile),
    }[step]


def plan(images, tile_rows, tile_cols, width):
    ext_rows, ext_cols = tile_rows + 2 * width, tile_cols + 2 * width
    own_count = images * tile_rows * tile_cols

    def own_at(n, i, j):
        return (n * tile_rows + i) * tile_cols + j

    def ext_at(n, i, j):
        return (i * images + n) * ext_cols + j

    pack, segments, placed = [], [], np.zeros(images * ext_rows * ext_cols, np.int64)
    for n in range(images):
        for i in range(tile_rows):
            for j in range(tile_cols):
                placed[ext_at(n, i + width, j + width)] = own_at(n, i, j)
    for dr, dc in SIDES:
        start = len(pack)
        pairs = zip(edge_source(dr, tile_rows, width), edge_target(dr, tile_rows, width))
        for i, ti in pairs:
            for n in range(images):
                cols = zip(edge_source(dc, tile_cols, width), edge_target(dc, tile_cols, width))
                for j, tj in cols:
                    placed[ext_at(n, ti, tj)] = own_count + len(pack)
                    pack.append(own_at(n, i, j))
        segments.append((start, len(pack) - start))
    pack_matrix = np.eye(own_count)[np.array(pack)]
    place_matrix = np.eye(own_count + len(pack))[placed]
    read = np.zeros((own_count + own_count // 4, images * tile_rows * ext_cols))
    for n in range(images):
        for i in range(tile_rows):
            for j in range(tile_cols):
                at = ext_at(n, i, j + width)
                read[own_at(n, i, j), at] = 1.0
                token = (n * (tile_rows // 2) + i // 2) * (tile_cols // 2) + j // 2
                read[own_count + token, at] = 0.25
    return pack_matrix, place_matrix, read, segments


def dot(a, b):
    return jnp.dot(a, b, preferred_element_type=jnp.float32)


def dot_t(a, b):
    return lax.dot_general(a, b, (((1,), (1,)), ((), ())), preferred_element_type=jnp.float32)


def kernel(
    sizes,
    segments,
    own_ref, conv_hbm, gain_ref, qkv_hbm, qk_gain_ref, out_hbm, pack_ref, place_ref, read_ref,
    features_ref, mixed_ref,
    conv_w, shifted_act, border, around, qkv_w, out_w, head_gain, pooled_own, pooled_all,
    tokens, terms, returned,
    conv_sem, local_sem, halo_send, halo_recv, weight_send, weight_recv,
    pool_send, pool_recv, back_send, back_recv,
):
    images, tile_rows, tile_cols, layers, row_count, col_count = sizes
    ext_rows, ext_cols = tile_rows + 2 * layers, tile_cols + 2 * layers
    channels = own_ref.shape[1]
    own_count = own_ref.shape[0]
    devices = row_count * col_count
    me_r, me_c = lax.axis_index("row"), lax.axis_index("col")
    me = me_r * col_count + me_c
    half = lax.rem(me_c, 2)
    head = me_c // 2
    partner = (me_r, me_c + 1 - 2 * half)

    def other(step):
        to = lax.rem(me + step, devices)
        return to // col_count, lax.rem(to, col_count)

    barrier = pltpu.get_barrier_semaphore()

    def greet(step, _):
        pl.semaphore_signal(barrier, inc=1, device_id=other(step), device_id_type=MESH)
        return 0

    lax.fori_loop(1, devices, greet, 0)
    own_qkv = pltpu.make_async_copy(qkv_hbm, qkv_w.at[half], local_sem.at[0])
    own_out = pltpu.make_async_copy(out_hbm, out_w.at[half], local_sem.at[1])
    own_qkv.start()
    own_out.start()
    conv_copies = []
    for layer in range(layers):
        for a in range(3):
            at = layer * 3 + a
            copy = pltpu.make_async_copy(conv_hbm.at[layer, a], conv_w.at[layer, a], conv_sem.at[at])
            copy.start()
            conv_copies.append(copy)

    border[...] = dot(pack_ref[...], own_ref[...]).astype(jnp.bfloat16)
    around[:own_count] = own_ref[...]
    head_gain[half] = jnp.zeros(head_gain.shape[1:], jnp.float32)
    head_gain[half, :2, : qk_gain_ref.shape[1]] = qk_gain_ref[...].astype(jnp.float32)
    pl.semaphore_wait(barrier, devices - 1)

    halo_copies = []
    for k, (dr, dc) in enumerate(SIDES):
        start, count = segments[k]
        to = (lax.rem(me_r + dr + row_count, row_count), lax.rem(me_c + dc + col_count, col_count))
        copy = pltpu.make_async_remote_copy(
            src_ref=border.at[pl.ds(start, count)],
            dst_ref=around.at[pl.ds(own_count + start, count)],
            send_sem=halo_send.at[k],
            recv_sem=halo_recv.at[k],
            device_id=to,
            device_id_type=MESH,
        )
        copy.start()
        halo_copies.append(copy)
    own_qkv.wait()
    own_out.wait()
    weight_copies = []
    for k, ref in enumerate((qkv_w, out_w, head_gain)):
        copy = pltpu.make_async_remote_copy(
            src_ref=ref.at[half],
            dst_ref=ref.at[half],
            send_sem=weight_send.at[k],
            recv_sem=weight_recv.at[k],
            device_id=partner,
            device_id_type=MESH,
        )
        copy.start()
        weight_copies.append(copy)
    for copy in halo_copies:
        copy.wait_recv()

    hidden = dot(place_ref[...], around[...])
    line = images * ext_cols
    for layer in range(layers):
        factor = lax.rsqrt(jnp.mean(hidden * hidden, axis=-1, keepdims=True) + 1e-06)
        act = jax.nn.silu(hidden * factor * gain_ref[layer : layer + 1, :])
        rows = act.shape[0]
        groups = act.reshape(rows // ext_cols, ext_cols, channels)
        for b in range(3):
            moved = groups if b == 1 else pltpu.roll(groups, (1 - b) % ext_cols, axis=1)
            shifted_act[b, :rows] = moved.reshape(rows, channels).astype(jnp.bfloat16)
        inner = rows - 2 * line
        total = jnp.zeros((inner, channels), jnp.float32)
        for a in range(3):
            conv_copies[layer * 3 + a].wait()
            for b in range(3):
                total = total + dot(shifted_act[b, a * line : a * line + inner], conv_w[layer, a, b])
        rounded = (hidden[line : line + inner] + total).astype(jnp.bfloat16)
        hidden = rounded.astype(jnp.float32)

    both = dot(read_ref[...], rounded)
    features_ref[...] = both[:own_count].astype(jnp.bfloat16)
    pooled = both[own_count:].astype(jnp.bfloat16).astype(jnp.float32)
    tile_tokens = pooled_own.shape[1]
    for n in range(images):
        pooled_own[n] = pooled[n * tile_tokens : (n + 1) * tile_tokens]

    slot = me_c * row_count + me_r

    def scatter(step, _):
        to = other(step)
        pltpu.make_async_remote_copy(
            src_ref=pooled_own.at[to[0]],
            dst_ref=pooled_all.at[slot],
            send_sem=pool_send,
            recv_sem=pool_recv,
            device_id=to,
            device_id_type=MESH,
        ).start()
        return 0

    lax.fori_loop(1, devices, scatter, 0)
    pooled_all[slot] = pooled_own[me_r]
    for copy in weight_copies:
        copy.wait_recv()
    arrived = pltpu.make_async_remote_copy(
        src_ref=pooled_all.at[pl.ds(0, devices - 1)],
        dst_ref=pooled_all.at[pl.ds(0, devices - 1)],
        send_sem=pool_send,
        recv_sem=pool_recv,
        device_id=partner,
        device_id_type=MESH,
    )
    arrived.wait_recv()

    def join(i):
        return jnp.concatenate([pooled_all[2 * i], pooled_all[2 * i + 1]], axis=0)

    if devices <= 64:
        for i in range(devices // 2):
            tokens[8 * i : 8 * i + 8] = join(i)
    else:

        def put(i, _):
            tokens[pl.ds(pl.multiple_of(8 * i, 8), 8)] = join(i)
            return 0

        lax.fori_loop(0, devices // 2, put, 0)

    head_dim = 2 * qkv_w.shape[2]

    def head_matrix(part):
        return qkv_w[:, part].reshape(head_dim, channels)

    gains = head_gain[0] + pltpu.roll(head_gain[1], head_dim // 2, axis=1)

    def head_norm(projected, gain_row):
        factor = lax.rsqrt(jnp.mean(projected * projected, axis=-1, keepdims=True) + 1e-06)
        return (projected * factor * gain_row).astype(jnp.bfloat16)

    count = tokens.shape[0]
    queries = count // 2
    image_tokens = tokens[...].astype(jnp.bfloat16)
    key_norm = head_norm(dot_t(image_tokens, head_matrix(1)), gains[1:2])
    value_rows = dot_t(image_tokens, head_matrix(2)).astype(jnp.bfloat16)
    block = min(queries, 128)
    strip = terms.shape[1]

    def attend(at):
        first = half * queries + at * block
        rows = tokens[pl.ds(pl.multiple_of(first, block), block)].astype(jnp.bfloat16)
        query_norm = head_norm(dot_t(rows, head_matrix(0)), gains[0:1])
        scores = dot_t(query_norm, key_norm) * head_dim ** (-0.5)
        shifted = jnp.exp(scores - jnp.max(scores, axis=1, keepdims=True))
        out = dot(shifted.astype(jnp.bfloat16), value_rows)
        return (out / jnp.sum(shifted, axis=1, keepdims=True)).astype(jnp.bfloat16)

    out_rows = out_w[...].reshape(head_dim, channels)

    def one_block(at):
        term = dot(attend(at), out_rows).astype(jnp.bfloat16)
        for k in range(block // strip):
            terms[at * (block // strip) + k] = term[k * strip : (k + 1) * strip]

    if queries == block:
        one_block(0)
    else:

        def step(at, _):
            one_block(at)
            return 0

        lax.fori_loop(0, queries // block, step, 0)

    heads = col_count // 2

    def back(k):
        return pltpu.make_async_remote_copy(
            src_ref=terms.at[k],
            dst_ref=returned.at[head],
            send_sem=back_send.at[k],
            recv_sem=back_recv.at[head],
            device_id=(me_r, half * heads + k),
            device_id_type=MESH,
        )

    for k in range(heads):

        @pl.when(half * heads + k != me_c)
        def _():
            back(k).start()

        @pl.when(half * heads + k == me_c)
        def _():
            returned[head] = terms[k]

    mine = tokens[pl.ds(pl.multiple_of(me_c * strip, strip), strip)]
    for h in range(heads):

        @pl.when(2 * h + me_c // heads != me_c)
        def _():
            pltpu.make_async_remote_copy(
                src_ref=terms.at[0],
                dst_ref=returned.at[h],
                send_sem=back_send.at[0],
                recv_sem=back_recv.at[h],
                device_id=partner,
                device_id_type=MESH,
            ).wait_recv()

    total = returned[0].astype(jnp.float32)
    for h in range(1, heads):
        total = total + returned[h].astype(jnp.float32)
    mixed_ref[...] = (mine + total).astype(jnp.bfloat16)

    for copy in halo_copies + weight_copies:
        copy.wait_send()
    arrived.wait_send()
    for k in range(heads):

        @pl.when(half * heads + k != me_c)
        def _():
            back(k).wait_send()


def shards(latent, conv_weight, conv_gain, qkv_weight, qk_gain, out_weight):
    images, tile_rows, tile_cols, channels = latent.shape
    layers = conv_weight.shape[0]
    row_count, col_count = lax.axis_size("row"), lax.axis_size("col")
    devices = row_count * col_count
    sizes = (images, tile_rows, tile_cols, layers, row_count, col_count)
    pack, place, read, segments = plan(images, tile_rows, tile_cols, layers)
    own_count, border_count = pack.shape[1], pack.shape[0]
    tile_tokens = tile_rows * tile_cols // 4
    image_tokens = devices * tile_tokens
    strip = row_count * tile_tokens
    heads = col_count // 2
    half_rows = qkv_weight.shape[1]
    ext_count = place.shape[0]
    bf16, f32 = jnp.bfloat16, jnp.float32
    vmem, anywhere = pl.BlockSpec(memory_space=pltpu.VMEM), pl.BlockSpec(memory_space=pl.ANY)
    dma = pltpu.SemaphoreType.DMA
    features, mixed = pl.pallas_call(
        functools.partial(kernel, sizes, segments),
        out_shape=(
            jax.ShapeDtypeStruct((own_count, channels), bf16),
            jax.ShapeDtypeStruct((strip, channels), bf16),
        ),
        in_specs=[vmem, anywhere, vmem, anywhere, vmem, anywhere, vmem, vmem, vmem],
        out_specs=(vmem, vmem),
        scratch_shapes=[
            pltpu.VMEM(conv_weight.shape, bf16),
            pltpu.VMEM((3, ext_count, channels), bf16),
            pltpu.VMEM((border_count, channels), bf16),
            pltpu.VMEM((own_count + border_count, channels), bf16),
            pltpu.VMEM((2,) + qkv_weight.shape, bf16),
            pltpu.VMEM((2,) + out_weight.shape, bf16),
            pltpu.VMEM((2, 8, 2 * half_rows), f32),
            pltpu.VMEM((images, tile_tokens, channels), f32),
            pltpu.VMEM((devices, tile_tokens, channels), f32),
            pltpu.VMEM((image_tokens, channels), f32),
            pltpu.VMEM((heads, strip, channels), bf16),
            pltpu.VMEM((heads, strip, channels), bf16),
            dma((layers * 3,)),
            dma((2,)),
            dma((len(SIDES),)),
            dma((len(SIDES),)),
            dma((3,)),
            dma((3,)),
            dma,
            dma,
            dma((heads,)),
            dma((heads,)),
        ],
        compiler_params=pltpu.CompilerParams(
            collective_id=0, has_side_effects=True, vmem_limit_bytes=56 * 1024 * 1024
        ),
    )(
        latent.reshape(own_count, channels),
        conv_weight,
        conv_gain,
        qkv_weight,
        qk_gain,
        out_weight,
        jnp.asarray(pack, bf16),
        jnp.asarray(place, bf16),
        jnp.asarray(read, bf16),
    )
    return (
        features.reshape(latent.shape),
        mixed.reshape(1, row_count * tile_rows // 2, tile_cols // 2, channels),
    )


def solution(mesh):
    placed = (
        P(None, "row", "col", None),
        P(),
        P(),
        P(None, "col", None),
        P(None, "col"),
        P("col", None),
    )
    return jax.shard_map(
        shards,
        mesh=mesh,
        in_specs=placed,
        out_specs=(P(None, "row", "col", None), P("row", None, "col", None)),
        check_vma=False,
    )
```

time: 91.2 us -> 32.4 us (0.36)
  blocking collectives: 30.6 us -> 0 us
  Pallas kernels: 0 us -> 27.2 us
  starting transfers between devices: 20.8 us -> 0 us
  waiting for transfers between devices: 11.1 us -> 0 us
  local copies, waits for them, and re-layouts: 14.4 us -> 4.2 us
  matrix products: 8.97 us -> 0 us
  other arithmetic: 3.73 us -> 0 us
    all_gather x1 -> x0, blocking collectives: 30.6 us -> none  [shards(): image_tok = lax.all_gather(own_strip, 'col', axis=1, tiled=True)]
    pallas_call x0 -> x1, Pallas kernels: none -> 27.2 us  [shards(): pl.pallas_call(functools.partial(kernel, sizes, segments), out_shape=(jax...]
    ppermute x7 -> x0, starting transfers between devices: 11.5 us -> none  [the longest x2 6.71 us: with_halo(): after = lax.ppermute(leading, axis, down)]
    all_to_all x2 -> x0, waiting for transfers between devices: 9.61 us -> none  [the longest x1 6.76 us: shards(): lax.all_to_all(head_terms.astype(jnp.bfloat16), 'col', split_axis=1, conc...]
    all_to_all x2 -> x0, starting transfers between devices: 9.24 us -> none  [the longest x1 5.99 us: shards(): lax.all_to_all(head_terms.astype(jnp.bfloat16), 'col', split_axis=1, conc...]
    dot_general x23 -> x0, matrix products: 8.97 us -> none  [the longest x18 7.63 us: conv_taps(): jnp.dot(window.reshape(image_count * out_rows * out_cols, channels), kern...]
    squeeze x2 -> x0, local copies, waits for them, and re-layouts: 4.12 us -> none  [the longest x1 4.12 us: shards(): conv_weight[layer_index]]
    slice x5 -> x0, local copies, waits for them, and re-layouts: 2.57 us -> none  [the longest x2 0.94 us: conv_taps(): window = padded[:, row_tap:row_tap + out_rows, col_tap:col_tap + out_cols]]
  transfers between devices with their start and end apart: 9 -> 0, of which waited for: 3 -> 0; matrix products, arithmetic and copies ran while one was open for 25% -> 0% of each run, Pallas kernels for 0% -> 0%
where the time goes in v1:
time: 32.4 us; the launch traced here: 32.1 us
  Pallas kernels  27.2 us (84%)
  local copies, waits for them, and re-layouts  4.2 us (13%)
  between operations  0.64 us (2%)
    pallas_call x1, Pallas kernels, shards(): pl.pallas_call(functools.partial(kernel, sizes, segments), out_shape=(jax...  27.2 us
    reshape x1, local copies, waits for them, and re-layouts, shards(): latent.reshape(own_count, channels)  1.45 us
    reshape x1, local copies, waits for them, and re-layouts, shards(): features.reshape(latent.shape)  1.44 us
    reshape x1, local copies, waits for them, and re-layouts, shards(): mixed.reshape(1, row_count * tile_rows // 2, tile_cols // 2, channels)  1.32 us

profile of v1, /device:TPU:0, one launch (start us, length us, event | category | flops | bytes accessed | tf_op | source)
XLA Modules:
  0.0 32.1 jit_solution(6034190153306689301)
XLA Ops:
  0.6 1.4 %reshape.13.own_ref = bf16[64,320]{1,0:T(8,128)(2,1)} reshape(bf16[4,4,4,320]{3,2,1,0:T(4,128)(2,1)} %param.9) | data formatting | bytes 81920 | tf_op jit(solution)/shard_map/reshape | solution.py:371
  2.1 27.2 %shard_map.104 = (bf16[64,320]{1,0:T(8,128)(2,1)}, bf16[16,320]{1,0:T(8,128)(2,1)}) custom-call(bf16[64,320]{1,0:T(8,128)(2,1)} %reshape.13.own_ref, bf16[2,3,3,320,320]{4,3,2,1,0:T(8,128)(2,1)} %conv_hbm.1, f32[2,320]{1,0:T(2,128)} %gain_ref.1, bf16[3,64,320]{2,1,0:T(8,128)(2,1)} %qkv_hbm.1, bf16[2,64]{1,0:T(2,128)(2,1)} %qk_gain_ref.1, ...), custom_call_target="tpu_custom_call" | custom-call | tf_op jit(solution)/shard_map/pallas_call | solution.py:335
  29.3 1.4 %reshape.14 = bf16[4,4,4,320]{3,2,1,0:T(4,128)(2,1)} reshape(bf16[64,320]{1,0:T(8,128)(2,1)} %get-tuple-element.4) | data formatting | bytes 81920 | tf_op jit(solution)/shard_map/reshape | solution.py:382
  30.8 1.3 %reshape.15 = bf16[1,8,2,320]{3,2,1,0:T(2,128)(2,1)} reshape(bf16[16,320]{1,0:T(8,128)(2,1)} %get-tuple-element.5) | data formatting | bytes 20480 | tf_op jit(solution)/shard_map/reshape | solution.py:383

commit v2 on v1

--- a/solution.py
+++ b/solution.py
@@ -73,35 +73,36 @@
 def kernel(
     sizes,
     segments,
-    own_ref, conv_hbm, gain_ref, qkv_hbm, qk_gain_ref, out_hbm, pack_ref, place_ref, read_ref,
-    features_ref, mixed_ref,
-    conv_w, shifted_act, border, around, qkv_w, out_w, head_gain, pooled_own, pooled_all,
-    tokens, terms, returned,
-    conv_sem, local_sem, halo_send, halo_recv, weight_send, weight_recv,
-    pool_send, pool_recv, back_send, back_recv,
+    latent_ref, conv_hbm, gain_ref, qkv_hbm, qk_gain_ref, out_hbm, pack_ref, place_ref, read_ref,
+    features_hbm, mixed_hbm,
+    conv_w, shifted_act, border, around, qkv_w, out_w, head_gain, pooled_own, pooled_row,
+    strips, terms, returned, own_rows, features, mixed,
+    conv_sem, local_sem, out_sem, halo_send, halo_recv, weight_send, weight_recv,
+    row_send, row_recv, col_send, col_recv, back_send, back_recv,
 ):
     images, tile_rows, tile_cols, layers, row_count, col_count = sizes
     ext_rows, ext_cols = tile_rows + 2 * layers, tile_cols + 2 * layers
-    channels = own_ref.shape[1]
-    own_count = own_ref.shape[0]
-    devices = row_count * col_count
+    channels = latent_ref.shape[-1]
+    own_count = images * tile_rows * tile_cols
     me_r, me_c = lax.axis_index("row"), lax.axis_index("col")
-    me = me_r * col_count + me_c
     half = lax.rem(me_c, 2)
     head = me_c // 2
     partner = (me_r, me_c + 1 - 2 * half)
 
-    def other(step):
-        to = lax.rem(me + step, devices)
-        return to // col_count, lax.rem(to, col_count)
+    def in_row(step):
+        return lax.rem(me_r + step, row_count), me_c
+
+    def in_col(step):
+        return me_r, lax.rem(me_c + step, col_count)
 
     barrier = pltpu.get_barrier_semaphore()
 
-    def greet(step, _):
-        pl.semaphore_signal(barrier, inc=1, device_id=other(step), device_id_type=MESH)
-        return 0
-
-    lax.fori_loop(1, devices, greet, 0)
+    peers = [in_row(step) for step in range(1, row_count)]
+    peers += [in_col(step) for step in range(1, col_count)]
+    for dr, dc in SIDES[4:]:
+        peers.append((in_row(row_count + dr)[0], in_col(col_count + dc)[1]))
+    for peer in peers:
+        pl.semaphore_signal(barrier, inc=1, device_id=peer, device_id_type=MESH)
     own_qkv = pltpu.make_async_copy(qkv_hbm, qkv_w.at[half], local_sem.at[0])
     own_out = pltpu.make_async_copy(out_hbm, out_w.at[half], local_sem.at[1])
     own_qkv.start()
@@ -114,11 +115,16 @@
             copy.start()
             conv_copies.append(copy)
 
-    border[...] = dot(pack_ref[...], own_ref[...]).astype(jnp.bfloat16)
-    around[:own_count] = own_ref[...]
+    for n in range(images):
+        for i in range(tile_rows):
+            at = (n * tile_rows + i) * tile_cols
+            own_rows[at : at + tile_cols] = latent_ref[n, i].astype(jnp.float32)
+    own = own_rows[...].astype(jnp.bfloat16)
+    border[...] = dot(pack_ref[...], own).astype(jnp.bfloat16)
+    around[:own_count] = own
     head_gain[half] = jnp.zeros(head_gain.shape[1:], jnp.float32)
     head_gain[half, :2, : qk_gain_ref.shape[1]] = qk_gain_ref[...].astype(jnp.float32)
-    pl.semaphore_wait(barrier, devices - 1)
+    pl.semaphore_wait(barrier, len(peers))
 
     halo_copies = []
     for k, (dr, dc) in enumerate(SIDES):
@@ -171,53 +177,60 @@
         hidden = rounded.astype(jnp.float32)
 
     both = dot(read_ref[...], rounded)
-    features_ref[...] = both[:own_count].astype(jnp.bfloat16)
     pooled = both[own_count:].astype(jnp.bfloat16).astype(jnp.float32)
     tile_tokens = pooled_own.shape[1]
     for n in range(images):
         pooled_own[n] = pooled[n * tile_tokens : (n + 1) * tile_tokens]
 
-    slot = me_c * row_count + me_r
-
-    def scatter(step, _):
-        to = other(step)
+    for step in range(1, row_count):
+        to = in_row(step)
         pltpu.make_async_remote_copy(
             src_ref=pooled_own.at[to[0]],
-            dst_ref=pooled_all.at[slot],
-            send_sem=pool_send,
-            recv_sem=pool_recv,
+            dst_ref=pooled_row.at[me_r],
+            send_sem=row_send,
+            recv_sem=row_recv,
             device_id=to,
             device_id_type=MESH,
         ).start()
-        return 0
-
-    lax.fori_loop(1, devices, scatter, 0)
-    pooled_all[slot] = pooled_own[me_r]
-    for copy in weight_copies:
-        copy.wait_recv()
-    arrived = pltpu.make_async_remote_copy(
-        src_ref=pooled_all.at[pl.ds(0, devices - 1)],
-        dst_ref=pooled_all.at[pl.ds(0, devices - 1)],
-        send_sem=pool_send,
-        recv_sem=pool_recv,
+    pooled_row[me_r] = pooled_own[me_r]
+    for n in range(images):
+        for i in range(tile_rows):
+            at = (n * tile_rows + i) * tile_cols
+            features[n, i] = both[at : at + tile_cols].astype(jnp.bfloat16)
+    features_out = pltpu.make_async_copy(features, features_hbm, out_sem.at[0])
+    features_out.start()
+    row_arrived = pltpu.make_async_remote_copy(
+        src_ref=pooled_row.at[pl.ds(0, row_count - 1)],
+        dst_ref=pooled_row.at[pl.ds(0, row_count - 1)],
+        send_sem=row_send,
+        recv_sem=row_recv,
         device_id=partner,
         device_id_type=MESH,
     )
-    arrived.wait_recv()
-
-    def join(i):
-        return jnp.concatenate([pooled_all[2 * i], pooled_all[2 * i + 1]], axis=0)
-
-    if devices <= 64:
-        for i in range(devices // 2):
-            tokens[8 * i : 8 * i + 8] = join(i)
-    else:
-
-        def put(i, _):
-            tokens[pl.ds(pl.multiple_of(8 * i, 8), 8)] = join(i)
-            return 0
-
-        lax.fori_loop(0, devices // 2, put, 0)
+    row_arrived.wait_recv()
+
+    mine = jnp.concatenate([pooled_row[r] for r in range(row_count)], axis=0)
+    strips[me_c] = mine.astype(jnp.bfloat16)
+    for step in range(1, col_count):
+        pltpu.make_async_remote_copy(
+            src_ref=strips.at[me_c],
+            dst_ref=strips.at[me_c],
+            send_sem=col_send,
+            recv_sem=col_recv,
+            device_id=in_col(step),
+            device_id_type=MESH,
+        ).start()
+    for copy in weight_copies:
+        copy.wait_recv()
+    col_arrived = pltpu.make_async_remote_copy(
+        src_ref=strips.at[pl.ds(0, col_count - 1)],
+        dst_ref=strips.at[pl.ds(0, col_count - 1)],
+        send_sem=col_send,
+        recv_sem=col_recv,
+        device_id=partner,
+        device_id_type=MESH,
+    )
+    col_arrived.wait_recv()
 
     head_dim = 2 * qkv_w.shape[2]
 
@@ -230,17 +243,17 @@
         factor = lax.rsqrt(jnp.mean(projected * projected, axis=-1, keepdims=True) + 1e-06)
         return (projected * factor * gain_row).astype(jnp.bfloat16)
 
-    count = tokens.shape[0]
+    strip = terms.shape[1]
+    count = col_count * strip
     queries = count // 2
-    image_tokens = tokens[...].astype(jnp.bfloat16)
+    image_tokens = strips[...].reshape(count, channels)
     key_norm = head_norm(dot_t(image_tokens, head_matrix(1)), gains[1:2])
     value_rows = dot_t(image_tokens, head_matrix(2)).astype(jnp.bfloat16)
     block = min(queries, 128)
-    strip = terms.shape[1]
 
     def attend(at):
-        first = half * queries + at * block
-        rows = tokens[pl.ds(pl.multiple_of(first, block), block)].astype(jnp.bfloat16)
+        first = half * (col_count // 2) + at * (block // strip)
+        rows = strips[pl.ds(first, block // strip)].reshape(block, channels)
         query_norm = head_norm(dot_t(rows, head_matrix(0)), gains[0:1])
         scores = dot_t(query_norm, key_norm) * head_dim ** (-0.5)
         shifted = jnp.exp(scores - jnp.max(scores, axis=1, keepdims=True))
@@ -286,7 +299,6 @@
         def _():
             returned[head] = terms[k]
 
-    mine = tokens[pl.ds(pl.multiple_of(me_c * strip, strip), strip)]
     for h in range(heads):
 
         @pl.when(2 * h + me_c // heads != me_c)
@@ -303,28 +315,35 @@
     total = returned[0].astype(jnp.float32)
     for h in range(1, heads):
         total = total + returned[h].astype(jnp.float32)
-    mixed_ref[...] = (mine + total).astype(jnp.bfloat16)
+    total = mine + total
+    for t in range(mixed.shape[1]):
+        width = mixed.shape[2]
+        mixed[0, t] = total[t * width : (t + 1) * width].astype(jnp.bfloat16)
+    mixed_out = pltpu.make_async_copy(mixed, mixed_hbm, out_sem.at[1])
+    mixed_out.start()
 
     for copy in halo_copies + weight_copies:
         copy.wait_send()
-    arrived.wait_send()
+    row_arrived.wait_send()
+    col_arrived.wait_send()
     for k in range(heads):
 
         @pl.when(half * heads + k != me_c)
         def _():
             back(k).wait_send()
+
+    features_out.wait()
+    mixed_out.wait()
 
 
 def shards(latent, conv_weight, conv_gain, qkv_weight, qk_gain, out_weight):
     images, tile_rows, tile_cols, channels = latent.shape
     layers = conv_weight.shape[0]
     row_count, col_count = lax.axis_size("row"), lax.axis_size("col")
-    devices = row_count * col_count
     sizes = (images, tile_rows, tile_cols, layers, row_count, col_count)
     pack, place, read, segments = plan(images, tile_rows, tile_cols, layers)
     own_count, border_count = pack.shape[1], pack.shape[0]
     tile_tokens = tile_rows * tile_cols // 4
-    image_tokens = devices * tile_tokens
     strip = row_count * tile_tokens
     heads = col_count // 2
     half_rows = qkv_weight.shape[1]
@@ -332,14 +351,15 @@
     bf16, f32 = jnp.bfloat16, jnp.float32
     vmem, anywhere = pl.BlockSpec(memory_space=pltpu.VMEM), pl.BlockSpec(memory_space=pl.ANY)
     dma = pltpu.SemaphoreType.DMA
-    features, mixed = pl.pallas_call(
+    mixed_shape = (1, row_count * tile_rows // 2, tile_cols // 2, channels)
+    return pl.pallas_call(
         functools.partial(kernel, sizes, segments),
         out_shape=(
-            jax.ShapeDtypeStruct((own_count, channels), bf16),
-            jax.ShapeDtypeStruct((strip, channels), bf16),
+            jax.ShapeDtypeStruct(latent.shape, bf16),
+            jax.ShapeDtypeStruct(mixed_shape, bf16),
         ),
         in_specs=[vmem, anywhere, vmem, anywhere, vmem, anywhere, vmem, vmem, vmem],
-        out_specs=(vmem, vmem),
+        out_specs=(anywhere, anywhere),
         scratch_shapes=[
             pltpu.VMEM(conv_weight.shape, bf16),
             pltpu.VMEM((3, ext_count, channels), bf16),
@@ -349,16 +369,22 @@
             pltpu.VMEM((2,) + out_weight.shape, bf16),
             pltpu.VMEM((2, 8, 2 * half_rows), f32),
             pltpu.VMEM((images, tile_tokens, channels), f32),
-            pltpu.VMEM((devices, tile_tokens, channels), f32),
-            pltpu.VMEM((image_tokens, channels), f32),
+            pltpu.VMEM((row_count, tile_tokens, channels), f32),
+            pltpu.VMEM((col_count, strip, channels), bf16),
             pltpu.VMEM((heads, strip, channels), bf16),
             pltpu.VMEM((heads, strip, channels), bf16),
+            pltpu.VMEM((own_count, channels), f32),
+            pltpu.VMEM(latent.shape, bf16),
+            pltpu.VMEM(mixed_shape, bf16),
             dma((layers * 3,)),
+            dma((2,)),
             dma((2,)),
             dma((len(SIDES),)),
             dma((len(SIDES),)),
             dma((3,)),
             dma((3,)),
+            dma,
+            dma,
             dma,
             dma,
             dma((heads,)),
@@ -368,7 +394,7 @@
             collective_id=0, has_side_effects=True, vmem_limit_bytes=56 * 1024 * 1024
         ),
     )(
-        latent.reshape(own_count, channels),
+        latent,
         conv_weight,
         conv_gain,
         qkv_weight,
@@ -377,10 +403,6 @@
         jnp.asarray(pack, bf16),
         jnp.asarray(place, bf16),
         jnp.asarray(read, bf16),
-    )
-    return (
-        features.reshape(latent.shape),
-        mixed.reshape(1, row_count * tile_rows // 2, tile_cols // 2, channels),
     )
 
 

time: 32.4 us -> 30.9 us (0.954)
  local copies, waits for them, and re-layouts: 4.2 us -> 2.75 us
    reshape x3 -> x0, local copies, waits for them, and re-layouts: 4.2 us -> none  [the longest x1 1.45 us: shards(): latent.reshape(own_count, channels)]
    unnamed x0 -> x2, local copies, waits for them, and re-layouts: none -> 2.75 us
where the time goes in v2:
time: 30.9 us; the launch traced here: 30.7 us
  Pallas kernels  27.3 us (88%)
  local copies, waits for them, and re-layouts  2.75 us (9%)
  between operations  0.64 us (2%)
    pallas_call x1, Pallas kernels, shards(): pl.pallas_call(functools.partial(kernel, sizes, segments), out_shape=(jax...  27.3 us
    unnamed x2, local copies, waits for them, and re-layouts  2.75 us

profile of v2, /device:TPU:0, one launch (start us, length us, event | category | flops | bytes accessed | tf_op | source)
XLA Modules:
  0.0 30.7 jit_solution(15406147547864454295)
XLA Ops:
  0.6 27.3 %shard_map.104 = (bf16[4,4,4,320]{3,2,1,0:T(4,128)(2,1)}, bf16[1,8,2,320]{3,2,1,0:T(2,128)(2,1)}) custom-call(bf16[4,4,4,320]{3,2,1,0:T(4,128)(2,1)} %latent_ref.1, bf16[2,3,3,320,320]{4,3,2,1,0:T(8,128)(2,1)} %conv_hbm.1, f32[2,320]{1,0:T(2,128)} %gain_ref.1, bf16[3,64,320]{2,1,0:T(8,128)(2,1)} %qkv_hbm.1, bf16[2,64]{1,0:T(2,128)(2,1)} %qk_gain_ref.1, ...), custom_call_target="tpu_custom_call" | custom-call | tf_op jit(solution)/shard_map/pallas_call | solution.py:355
  27.9 1.4 %copy.13 = bf16[4,4,4,320]{3,2,1,0:T(4,128)(2,1)} copy(bf16[4,4,4,320]{3,2,1,0:T(4,128)(2,1)} %get-tuple-element.4) | data formatting | bytes 81920
  29.4 1.3 %copy.14 = bf16[1,8,2,320]{3,2,1,0:T(2,128)(2,1)} copy(bf16[1,8,2,320]{3,2,1,0:T(2,128)(2,1)} %get-tuple-element.5) | data formatting | bytes 20480

commit v3 on v2

--- a/solution.py
+++ b/solution.py
@@ -84,6 +84,7 @@
     ext_rows, ext_cols = tile_rows + 2 * layers, tile_cols + 2 * layers
     channels = latent_ref.shape[-1]
     own_count = images * tile_rows * tile_cols
+    lanes = conv_w.shape[2] // 3
     me_r, me_c = lax.axis_index("row"), lax.axis_index("col")
     half = lax.rem(me_c, 2)
     head = me_c // 2
@@ -110,10 +111,20 @@
     conv_copies = []
     for layer in range(layers):
         for a in range(3):
-            at = layer * 3 + a
-            copy = pltpu.make_async_copy(conv_hbm.at[layer, a], conv_w.at[layer, a], conv_sem.at[at])
-            copy.start()
-            conv_copies.append(copy)
+            for b in range(3):
+                copy = pltpu.make_async_copy(
+                    conv_hbm.at[layer, a, b],
+                    conv_w.at[layer, a, pl.ds(b * lanes, channels)],
+                    conv_sem.at[len(conv_copies)],
+                )
+                copy.start()
+                conv_copies.append(copy)
+                if lanes > channels:
+                    conv_w[layer, a, b * lanes + channels : (b + 1) * lanes] = jnp.zeros(
+                        (lanes - channels, channels), jnp.bfloat16
+                    )
+    if lanes > channels:
+        shifted_act[...] = jnp.zeros_like(shifted_act)
 
     for n in range(images):
         for i in range(tile_rows):
@@ -166,13 +177,15 @@
         groups = act.reshape(rows // ext_cols, ext_cols, channels)
         for b in range(3):
             moved = groups if b == 1 else pltpu.roll(groups, (1 - b) % ext_cols, axis=1)
-            shifted_act[b, :rows] = moved.reshape(rows, channels).astype(jnp.bfloat16)
+            shifted_act[:rows, b * lanes : b * lanes + channels] = moved.reshape(
+                rows, channels
+            ).astype(jnp.bfloat16)
         inner = rows - 2 * line
         total = jnp.zeros((inner, channels), jnp.float32)
         for a in range(3):
-            conv_copies[layer * 3 + a].wait()
             for b in range(3):
-                total = total + dot(shifted_act[b, a * line : a * line + inner], conv_w[layer, a, b])
+                conv_copies[(layer * 3 + a) * 3 + b].wait()
+            total = total + dot(shifted_act[a * line : a * line + inner], conv_w[layer, a])
         rounded = (hidden[line : line + inner] + total).astype(jnp.bfloat16)
         hidden = rounded.astype(jnp.float32)
 
@@ -348,6 +361,7 @@
     heads = col_count // 2
     half_rows = qkv_weight.shape[1]
     ext_count = place.shape[0]
+    lanes = -(-channels // 128) * 128
     bf16, f32 = jnp.bfloat16, jnp.float32
     vmem, anywhere = pl.BlockSpec(memory_space=pltpu.VMEM), pl.BlockSpec(memory_space=pl.ANY)
     dma = pltpu.SemaphoreType.DMA
@@ -361,8 +375,8 @@
         in_specs=[vmem, anywhere, vmem, anywhere, vmem, anywhere, vmem, vmem, vmem],
         out_specs=(anywhere, anywhere),
         scratch_shapes=[
-            pltpu.VMEM(conv_weight.shape, bf16),
-            pltpu.VMEM((3, ext_count, channels), bf16),
+            pltpu.VMEM((layers, 3, 3 * lanes, channels), bf16),
+            pltpu.VMEM((ext_count, 3 * lanes), bf16),
             pltpu.VMEM((border_count, channels), bf16),
             pltpu.VMEM((own_count + border_count, channels), bf16),
             pltpu.VMEM((2,) + qkv_weight.shape, bf16),
@@ -376,7 +390,7 @@
             pltpu.VMEM((own_count, channels), f32),
             pltpu.VMEM(latent.shape, bf16),
             pltpu.VMEM(mixed_shape, bf16),
-            dma((layers * 3,)),
+            dma((layers * 9,)),
             dma((2,)),
             dma((2,)),
             dma((len(SIDES),)),

time: 30.9 us -> 30.6 us (level)
  no operation moved by 1% of the time
where the time goes in v3:
time: 30.6 us; the launch traced here: 30.4 us
  Pallas kernels  27 us (88%)
  local copies, waits for them, and re-layouts  2.75 us (9%)
  between operations  0.64 us (2%)
    pallas_call x1, Pallas kernels, shards(): pl.pallas_call(functools.partial(kernel, sizes, segments), out_shape=(jax...  27 us
    unnamed x2, local copies, waits for them, and re-layouts  2.75 us

profile of v3, /device:TPU:0, one launch (start us, length us, event | category | flops | bytes accessed | tf_op | source)
XLA Modules:
  0.0 30.4 jit_solution(17886943067256119978)
XLA Ops:
  0.6 27.0 %shard_map.104 = (bf16[4,4,4,320]{3,2,1,0:T(4,128)(2,1)}, bf16[1,8,2,320]{3,2,1,0:T(2,128)(2,1)}) custom-call(bf16[4,4,4,320]{3,2,1,0:T(4,128)(2,1)} %latent_ref.1, bf16[2,3,3,320,320]{4,3,2,1,0:T(8,128)(2,1)} %conv_hbm.1, f32[2,320]{1,0:T(2,128)} %gain_ref.1, bf16[3,64,320]{2,1,0:T(8,128)(2,1)} %qkv_hbm.1, bf16[2,64]{1,0:T(2,128)(2,1)} %qk_gain_ref.1, ...), custom_call_target="tpu_custom_call" | custom-call | tf_op jit(solution)/shard_map/pallas_call | solution.py:369
  27.6 1.4 %copy.13 = bf16[4,4,4,320]{3,2,1,0:T(4,128)(2,1)} copy(bf16[4,4,4,320]{3,2,1,0:T(4,128)(2,1)} %get-tuple-element.4) | data formatting | bytes 81920
  29.1 1.3 %copy.14 = bf16[1,8,2,320]{3,2,1,0:T(2,128)(2,1)} copy(bf16[1,8,2,320]{3,2,1,0:T(2,128)(2,1)} %get-tuple-element.5) | data formatting | bytes 20480

commit v4 on v3

--- a/solution.py
+++ b/solution.py
@@ -73,10 +73,11 @@
 def kernel(
     sizes,
     segments,
-    latent_ref, conv_hbm, gain_ref, qkv_hbm, qk_gain_ref, out_hbm, pack_ref, place_ref, read_ref,
+    latent_hbm, conv_hbm, gain_hbm, qkv_hbm, qk_gain_hbm, out_hbm, pack_hbm, place_hbm, read_hbm,
     features_hbm, mixed_hbm,
     conv_w, shifted_act, border, around, qkv_w, out_w, head_gain, pooled_own, pooled_row,
     strips, terms, returned, own_rows, features, mixed,
+    latent_ref, gain_ref, qk_gain_ref, pack_ref, place_ref, read_ref, small_sem,
     conv_sem, local_sem, out_sem, halo_send, halo_recv, weight_send, weight_recv,
     row_send, row_recv, col_send, col_recv, back_send, back_recv,
 ):
@@ -104,6 +105,18 @@
         peers.append((in_row(row_count + dr)[0], in_col(col_count + dc)[1]))
     for peer in peers:
         pl.semaphore_signal(barrier, inc=1, device_id=peer, device_id_type=MESH)
+    small_copies = []
+    for source, target in (
+        (latent_hbm, latent_ref),
+        (pack_hbm, pack_ref),
+        (qk_gain_hbm, qk_gain_ref),
+        (place_hbm, place_ref),
+        (gain_hbm, gain_ref),
+        (read_hbm, read_ref),
+    ):
+        copy = pltpu.make_async_copy(source, target, small_sem.at[len(small_copies)])
+        copy.start()
+        small_copies.append(copy)
     own_qkv = pltpu.make_async_copy(qkv_hbm, qkv_w.at[half], local_sem.at[0])
     own_out = pltpu.make_async_copy(out_hbm, out_w.at[half], local_sem.at[1])
     own_qkv.start()
@@ -125,6 +138,8 @@
                     )
     if lanes > channels:
         shifted_act[...] = jnp.zeros_like(shifted_act)
+    for copy in small_copies:
+        copy.wait()
 
     for n in range(images):
         for i in range(tile_rows):
@@ -363,7 +378,7 @@
     ext_count = place.shape[0]
     lanes = -(-channels // 128) * 128
     bf16, f32 = jnp.bfloat16, jnp.float32
-    vmem, anywhere = pl.BlockSpec(memory_space=pltpu.VMEM), pl.BlockSpec(memory_space=pl.ANY)
+    anywhere = pl.BlockSpec(memory_space=pl.ANY)
     dma = pltpu.SemaphoreType.DMA
     mixed_shape = (1, row_count * tile_rows // 2, tile_cols // 2, channels)
     return pl.pallas_call(
@@ -372,7 +387,7 @@
             jax.ShapeDtypeStruct(latent.shape, bf16),
             jax.ShapeDtypeStruct(mixed_shape, bf16),
         ),
-        in_specs=[vmem, anywhere, vmem, anywhere, vmem, anywhere, vmem, vmem, vmem],
+        in_specs=[anywhere] * 9,
         out_specs=(anywhere, anywhere),
         scratch_shapes=[
             pltpu.VMEM((layers, 3, 3 * lanes, channels), bf16),
@@ -390,6 +405,13 @@
             pltpu.VMEM((own_count, channels), f32),
             pltpu.VMEM(latent.shape, bf16),
             pltpu.VMEM(mixed_shape, bf16),
+            pltpu.VMEM(latent.shape, bf16),
+            pltpu.VMEM(conv_gain.shape, f32),
+            pltpu.VMEM(qk_gain.shape, bf16),
+            pltpu.VMEM(pack.shape, bf16),
+            pltpu.VMEM(place.shape, bf16),
+            pltpu.VMEM(read.shape, bf16),
+            dma((6,)),
             dma((layers * 9,)),
             dma((2,)),
             dma((2,)),

time: 30.6 us -> 29.9 us (0.977)
  Pallas kernels: 27 us -> 26.3 us
    pallas_call x1, Pallas kernels: 27 us -> 26.3 us  [shards(): pl.pallas_call(functools.partial(kernel, sizes, segments), out_shape=(jax...]
where the time goes in v4:
time: 29.9 us; the launch traced here: 29.7 us
  Pallas kernels  26.3 us (88%)
  local copies, waits for them, and re-layouts  2.75 us (9%)
  between operations  0.64 us (2%)
    pallas_call x1, Pallas kernels, shards(): pl.pallas_call(functools.partial(kernel, sizes, segments), out_shape=(jax...  26.3 us
    unnamed x2, local copies, waits for them, and re-layouts  2.75 us

profile of v4, /device:TPU:0, one launch (start us, length us, event | category | flops | bytes accessed | tf_op | source)
XLA Modules:
  0.0 29.7 jit_solution(7169802047402305312)
XLA Ops:
  0.6 26.3 %shard_map.104 = (bf16[4,4,4,320]{3,2,1,0:T(4,128)(2,1)}, bf16[1,8,2,320]{3,2,1,0:T(2,128)(2,1)}) custom-call(bf16[4,4,4,320]{3,2,1,0:T(4,128)(2,1)} %latent_hbm.1, bf16[2,3,3,320,320]{4,3,2,1,0:T(8,128)(2,1)} %conv_hbm.1, f32[2,320]{1,0:T(2,128)} %gain_hbm.1, bf16[3,64,320]{2,1,0:T(8,128)(2,1)} %qkv_hbm.1, bf16[2,64]{1,0:T(2,128)(2,1)} %qk_gain_hbm.1, ...), custom_call_target="tpu_custom_call" | custom-call | tf_op jit(solution)/shard_map/pallas_call | solution.py:384
  26.9 1.4 %copy.13 = bf16[4,4,4,320]{3,2,1,0:T(4,128)(2,1)} copy(bf16[4,4,4,320]{3,2,1,0:T(4,128)(2,1)} %get-tuple-element.4) | data formatting | bytes 81920
  28.4 1.3 %copy.14 = bf16[1,8,2,320]{3,2,1,0:T(2,128)(2,1)} copy(bf16[1,8,2,320]{3,2,1,0:T(2,128)(2,1)} %get-tuple-element.5) | data formatting | bytes 20480
